TPU v7x, 32 devices: a whole 2x2x4 slice. The times are simulated.
32 devices in a mesh: band: 8 (over z, x), slab: 4 (over y, core).
Axes of the slice: x: 2, y: 2, z: 4, core: 2. Of those that a mesh axis runs over, the one named last changes fastest.
Arguments:
- orbitals: float32 [32, 128, 128, 128], P('band', 'slab'), may hold values from -6 to 6
- owner_band: int32 [4], replicated, may hold values from 0 to 7
- owner_slot: int32 [4], replicated, may hold values from 0 to 3
- g_mask: int32 [128, 128, 128], P(None, 'slab'), may hold values from 0 to 1, as said below
Outputs:
- exchange_action: float32 [32, 128, 128, 128], P('band', 'slab')
Inputs may be any that keep to these rules, and one draw needn't show every extreme that they name: `owner_band`: the band index of the device that holds source orbital j. `owner_slot`: the position of source orbital j among its owner's 4 orbitals. 1 where the kernel is kept and 0 where it is cut; the point of zero wave vector, g_mask[0, 0, 0], is always cut.
All inputs are finite; a program needn't handle non-finite values.
Results may differ from a plain program's by a relative error of at most 0.0003.
Values sent between devices are 32-bit elements; how exact they have to be, the bound alone decides.
A program may use at most 192 MiB of HBM per device.

v0:
```python
import math
import jax
import jax.numpy as jnp
from jax import lax
from jax.sharding import PartitionSpec as P

GRID = 128
coulomb_gain = 128.0 * math.pi


def broadcast(value, axis, source):
    kept = jnp.where(lax.axis_index(axis) == source, value, 0).astype(value.dtype)
    return lax.psum(kept, axis)


def cas_matrix(count):
    wave_index = jnp.arange(count, dtype=jnp.int32)
    products = wave_index[:, None] * wave_index[None, :] % count
    angles = 2.0 * math.pi / count * products.astype(jnp.float32)
    return jnp.cos(angles) + jnp.sin(angles)


def fold_index(wave_index):
    return jnp.where(wave_index < GRID // 2, wave_index, wave_index - GRID).astype(jnp.float32)


def transform_planes(field, cas_rows):
    highest = lax.Precision.HIGHEST
    field = jnp.einsum("oxyz,kz->oxyk", field, cas_rows, precision=highest)
    return jnp.einsum("oxyz,ky->oxkz", field, cas_rows, precision=highest)


def transform_first(field, cas_rows):
    return jnp.einsum("oxyz,kx->okyz", field, cas_rows, precision=lax.Precision.HIGHEST)


def fetch_source(orbitals, owner_band, owner_slot, which):
    local_copy = lax.dynamic_index_in_dim(orbitals, owner_slot[which], 0, keepdims=False)
    return broadcast(local_copy, "band", owner_band[which])


def per_device(orbitals, owner_band, owner_slot, g_mask):
    cas_rows = cas_matrix(GRID)
    columns_dev = g_mask.shape[1]
    full_index = jnp.arange(GRID, dtype=jnp.int32)
    column_index = lax.axis_index("slab") * columns_dev + jnp.arange(columns_dev, dtype=jnp.int32)
    first_sq = fold_index(full_index) ** 2
    second_sq = fold_index(column_index) ** 2
    squares = first_sq[:, None, None] + second_sq[None, :, None] + first_sq[None, None, :]
    coulomb = g_mask.astype(jnp.float32) * coulomb_gain / (squares + 1.0)
    inverse = 1.0 / (GRID * GRID * GRID)
    source_count = owner_band.shape[0]
    sources = jnp.stack(
        [fetch_source(orbitals, owner_band, owner_slot, which) for which in range(source_count)]
    )
    accumulated = jnp.zeros(orbitals.shape, jnp.float32)
    for which in range(source_count):
        source_field = sources[which]
        density = orbitals * source_field[None]
        spectrum = transform_planes(density, cas_rows)
        items = lax.all_to_all(spectrum, "slab", split_axis=2, concat_axis=1, tiled=True)
        weigh_spectrum = transform_first(items, cas_rows) * coulomb[None]
        potential = transform_first(weigh_spectrum, cas_rows)
        potential = lax.all_to_all(potential, "slab", split_axis=1, concat_axis=2, tiled=True)
        potential = transform_planes(potential, cas_rows) * inverse
        accumulated = accumulated - potential * source_field[None]
    return accumulated


def solution(mesh):
    return jax.shard_map(
        per_device,
        mesh=mesh,
        in_specs=(P("band", "slab", None, None), P(), P(), P(None, "slab", None)),
        out_specs=P("band", "slab", None, None),
        check_vma=False,
    )
```

profile of v0, /device:TPU:0, one launch (start us, length us, event | category | flops | bytes accessed | tf_op | source)
XLA Modules:
  0.0 1164.9 jit_solution(12261178417186420591)
XLA Ops:
  27.2 275.4 %all-reduce.3.cloned.1.call-done = (f32[32,128,128]{2,1,0:T(8,128)}, f32[32,128,128]{2,1,0:T(8,128)}, f32[32,128,128]{2,1,0:T(8,128)}, f32[32,128,128]{2,1,0:T(8,128)}) async-done(((f32[32,128,128]{2,1,0:T(8,128)}, f32[32,128,128]{2,1,0:T(8,128)}, f32[32,128,128]{2,1,0:T(8,128)}, f32[32,128,128]{2,1,0:T(8,128)}), (f32[32,128,128]{2,1,0:T(8,128)}, f32[32,128,128]{2,1,0:T(8,128)}, f32[32,128,128]{2,1,0:T(8,128)}, ...) | async-done | bytes 8388624 | tf_op jit(solution)/shard_map/psum | solution.py:13
  302.5 10.5 fusion.30
  336.4 10.0 fusion.27
  363.5 66.1 %all-to-all-done = f32[4,32,128,128]{3,1,0,2:T(8,128)} async-done(((f32[4,32,128,128]{3,1,0,2:T(8,128)}), f32[4,32,128,128]{3,1,0,2:T(8,128)}, u32[]{:S(2)}, u32[]{:S(2)}) %all-to-all-start) | async-done | bytes 8388640 | tf_op jit(solution)/shard_map/all_to_all | solution.py:61
  435.2 10.0 fusion.24
  462.7 65.7 %all-to-all-done.2 = f32[4,32,128,128]{3,1,0,2:T(8,128)} async-done(((f32[4,32,128,128]{3,1,0,2:T(8,128)}), f32[4,32,128,128]{3,1,0,2:T(8,128)}, u32[]{:S(2)}, u32[]{:S(2)}) %all-to-all-start.2) | async-done | bytes 8388640 | tf_op jit(solution)/shard_map/all_to_all | solution.py:61
  534.1 10.0 fusion.21
  561.2 66.1 %all-to-all-done.4 = f32[4,32,128,128]{3,1,0,2:T(8,128)} async-done(((f32[4,32,128,128]{3,1,0,2:T(8,128)}), f32[4,32,128,128]{3,1,0,2:T(8,128)}, u32[]{:S(2)}, u32[]{:S(2)}) %all-to-all-start.4) | async-done | bytes 8388640 | tf_op jit(solution)/shard_map/all_to_all | solution.py:61
  635.0 9.9 copy.30
  644.9 12.7 %fusion.18 = f32[128,4,32,128]{3,0,2,1:T(8,128)S(1)} fusion(f32[4,128,32,128]{3,2,1,0:T(8,128)S(1)} %bitcast.172), kind=kOutput, calls=%fused_computation.22 | convolution fusion | flops 3221471232 | bytes 16777216 | tf_op jit(solution)/shard_map/oxyz,kx->okyz/dot_general | solution.py:34
  675.2 50.9 %all-to-all-done.6 = f32[4,32,128,128]{3,1,0,2:T(8,128)} async-done(((f32[4,32,128,128]{3,1,0,2:T(8,128)}), f32[4,32,128,128]{3,1,0,2:T(8,128)}, u32[]{:S(2)}, u32[]{:S(2)}) %all-to-all-start.6) | async-done | bytes 8388640 | tf_op jit(solution)/shard_map/all_to_all | solution.py:61
  731.9 9.9 copy.38
  741.8 12.6 %fusion.16 = f32[128,4,32,128]{3,0,2,1:T(8,128)S(1)} fusion(f32[4,128,32,128]{3,2,1,0:T(8,128)S(1)} %bitcast.173), kind=kOutput, calls=%fused_computation.20 | convolution fusion | flops 3221471232 | bytes 16777216 | tf_op jit(solution)/shard_map/oxyz,kx->okyz/dot_general | solution.py:34
  771.9 53.0 %all-to-all-done.1 = f32[4,128,32,128]{3,2,0,1:T(8,128)} async-done(((f32[4,128,32,128]{3,2,0,1:T(8,128)}), f32[4,128,32,128]{3,2,0,1:T(8,128)}, u32[]{:S(2)}, u32[]{:S(2)}) %all-to-all-start.1) | async-done | bytes 8388640 | tf_op jit(solution)/shard_map/all_to_all | solution.py:64
  840.6 12.6 %fusion.14 = f32[128,4,32,128]{3,0,2,1:T(8,128)S(1)} fusion(f32[4,128,32,128]{3,2,1,0:T(8,128)S(1)} %bitcast.174), kind=kOutput, calls=%fused_computation.18 | convolution fusion | flops 3221471232 | bytes 16777216 | tf_op jit(solution)/shard_map/oxyz,kx->okyz/dot_general | solution.py:34
  870.9 52.8 %all-to-all-done.3 = f32[4,128,32,128]{3,2,0,1:T(8,128)} async-done(((f32[4,128,32,128]{3,2,0,1:T(8,128)}), f32[4,128,32,128]{3,2,0,1:T(8,128)}, u32[]{:S(2)}, u32[]{:S(2)}) %all-to-all-start.3) | async-done | bytes 8388640 | tf_op jit(solution)/shard_map/all_to_all | solution.py:64
  939.4 12.7 %fusion.12 = f32[128,4,32,128]{3,0,2,1:T(8,128)S(1)} fusion(f32[4,128,32,128]{3,2,1,0:T(8,128)S(1)} %bitcast.175), kind=kOutput, calls=%fused_computation.16 | convolution fusion | flops 3221471232 | bytes 16777216 | tf_op jit(solution)/shard_map/oxyz,kx->okyz/dot_general | solution.py:34
  969.6 53.0 %all-to-all-done.5 = f32[4,128,32,128]{3,2,0,1:T(8,128)} async-done(((f32[4,128,32,128]{3,2,0,1:T(8,128)}), f32[4,128,32,128]{3,2,0,1:T(8,128)}, u32[]{:S(2)}, u32[]{:S(2)}) %all-to-all-start.5) | async-done | bytes 8388640 | tf_op jit(solution)/shard_map/all_to_all | solution.py:64
  1051.8 10.2 fusion.80
  1062.0 10.0 fusion.78
  1080.9 10.1 fusion.70
  1099.6 10.3 fusion.62
  1109.9 11.6 all-to-all-done.7
  1135.3 22.2 %fusion = f32[4,32,128,128]{3,2,1,0:T(8,128)} fusion(f32[128,4,32,128]{3,0,2,1:T(8,128)} %fusion.62, f32[128,4,32,128]{3,0,2,1:T(8,128)} %fusion.70, f32[128,4,32,128]{3,0,2,1:T(8,128)} %fusion.78, f32[32,128,128]{2,1,0:T(8,128)S(1)} %copy-done.6, f32[32,128,128]{2,1,0:T(8,128)} %get-tuple-element.22, f32[32,128,128]{2,1,0:T(8,128)} %get-tuple-element.23, ...), kind=kOutput, calls=%fused_computation.1 | convolution fusion | flops 3238248448 | bytes 50331648 | tf_op jit(solution)/shard_map/oxyz,ky->oxkz/dot_general | solution.py:30
  (61 shorter events, 272.2 us)
Async XLA Ops:
  6.5 296.0 %all-reduce.3.cloned.1.call-start = ((), (), s32[]{:S(2)}) async-start(), calls=%async_computation.8 | async-start | bytes 16777216 | tf_op jit(solution)/shard_map/psum | solution.py:13
  330.6 5.8 copy-start
  330.6 99.0 %all-to-all-start = ((f32[4,32,128,128]{3,1,0,2:T(8,128)}), f32[4,32,128,128]{3,1,0,2:T(8,128)}, u32[]{:S(2)}, u32[]{:S(2)}) async-start(f32[4,32,128,128]{3,1,0,2:T(8,128)} %copy.28), calls=%async_computation | async-start | bytes 16777216 | tf_op jit(solution)/shard_map/all_to_all | solution.py:61
  363.5 71.7 %copy-start.3 = (f32[32,128,128]{2,1,0:T(8,128)S(1)}, f32[32,128,128]{2,1,0:T(8,128)}, u32[]{:S(2)}) copy-start(f32[32,128,128]{2,1,0:T(8,128)} %get-tuple-element.5) | copy-start | bytes 6291460
  429.5 98.9 %all-to-all-start.2 = ((f32[4,32,128,128]{3,1,0,2:T(8,128)}), f32[4,32,128,128]{3,1,0,2:T(8,128)}, u32[]{:S(2)}, u32[]{:S(2)}) async-start(f32[4,32,128,128]{3,1,0,2:T(8,128)} %copy.36), calls=%async_computation.2 | async-start | bytes 16777216 | tf_op jit(solution)/shard_map/all_to_all | solution.py:61
  462.7 71.4 %copy-start.5 = (f32[32,128,128]{2,1,0:T(8,128)S(1)}, f32[32,128,128]{2,1,0:T(8,128)}, u32[]{:S(2)}) copy-start(f32[32,128,128]{2,1,0:T(8,128)} %get-tuple-element.8) | copy-start | bytes 6291460
  528.4 98.9 %all-to-all-start.4 = ((f32[4,32,128,128]{3,1,0,2:T(8,128)}), f32[4,32,128,128]{3,1,0,2:T(8,128)}, u32[]{:S(2)}, u32[]{:S(2)}) async-start(f32[4,32,128,128]{3,1,0,2:T(8,128)} %copy.43), calls=%async_computation.4 | async-start | bytes 16777216 | tf_op jit(solution)/shard_map/all_to_all | solution.py:61
  561.2 71.9 %copy-start.7 = (s32[128,32,128]{2,1,0:T(8,128)S(1)}, s32[128,32,128]{2,1,0:T(8,128)}, u32[]{:S(2)}) copy-start(s32[128,32,128]{2,1,0:T(8,128)} %param.7) | copy-start | bytes 6291460
  627.3 98.8 %all-to-all-start.6 = ((f32[4,32,128,128]{3,1,0,2:T(8,128)}), f32[4,32,128,128]{3,1,0,2:T(8,128)}, u32[]{:S(2)}, u32[]{:S(2)}) async-start(f32[4,32,128,128]{3,1,0,2:T(8,128)} %copy.50), calls=%async_computation.6 | async-start | bytes 16777216 | tf_op jit(solution)/shard_map/all_to_all | solution.py:61
  726.1 98.8 %all-to-all-start.1 = ((f32[4,128,32,128]{3,2,0,1:T(8,128)}), f32[4,128,32,128]{3,2,0,1:T(8,128)}, u32[]{:S(2)}, u32[]{:S(2)}) async-start(f32[4,128,32,128]{3,2,0,1:T(8,128)} %copy.33), calls=%async_computation.1 | async-start | bytes 16777216 | tf_op jit(solution)/shard_map/all_to_all | solution.py:64
  824.9 98.9 %all-to-all-start.3 = ((f32[4,128,32,128]{3,2,0,1:T(8,128)}), f32[4,128,32,128]{3,2,0,1:T(8,128)}, u32[]{:S(2)}, u32[]{:S(2)}) async-start(f32[4,128,32,128]{3,2,0,1:T(8,128)} %copy.40), calls=%async_computation.3 | async-start | bytes 16777216 | tf_op jit(solution)/shard_map/all_to_all | solution.py:64
  923.8 98.8 %all-to-all-start.5 = ((f32[4,128,32,128]{3,2,0,1:T(8,128)}), f32[4,128,32,128]{3,2,0,1:T(8,128)}, u32[]{:S(2)}, u32[]{:S(2)}) async-start(f32[4,128,32,128]{3,2,0,1:T(8,128)} %copy.47), calls=%async_computation.5 | async-start | bytes 16777216 | tf_op jit(solution)/shard_map/all_to_all | solution.py:64
  969.6 58.8 %copy-start.4 = (f32[32,128,128]{2,1,0:T(8,128)S(1)}, f32[32,128,128]{2,1,0:T(8,128)}, u32[]{:S(2)}) copy-start(f32[32,128,128]{2,1,0:T(8,128)} %get-tuple-element.5) | copy-start | bytes 6291460
  1022.5 99.0 %all-to-all-start.7 = ((f32[4,128,32,128]{3,2,0,1:T(8,128)}), f32[4,128,32,128]{3,2,0,1:T(8,128)}, u32[]{:S(2)}, u32[]{:S(2)}) async-start(f32[4,128,32,128]{3,2,0,1:T(8,128)} %copy.54), calls=%async_computation.7 | async-start | bytes 16777216 | tf_op jit(solution)/shard_map/all_to_all | solution.py:64
  1028.4 4.1 copy-start.1
  1028.4 4.1 copy-start.2
  1125.9 9.4 copy-start.6
Sparse Core Ops, SparseCore 0:
  27.3 275.2 all-reduce.2
where the time goes:
time: 1170 us; the launch traced here: 1160 us
  waiting for transfers between devices  695 us (59%)
  matrix products  253 us (22%)
  local copies, waits for them, and re-layouts  132 us (11%)
  starting transfers between devices  46 us (4%)
  between operations  24.4 us (2%)
  other arithmetic  14.7 us (1%)
    psum x1, waiting for transfers between devices, broadcast(): return lax.psum(kept, axis)  275 us
    all_to_all x4, waiting for transfers between devices, per_device(): lax.all_to_all(spectrum, 'slab', split_axis=2, concat_axis=1, tiled=True)  249 us
    all_to_all x4, waiting for transfers between devices, per_device(): lax.all_to_all(potential, 'slab', split_axis=1, concat_axis=2, tiled=True)  170 us
    dot_general x8, matrix products, transform_first(): jnp.einsum('oxyz,kx->okyz', field, cas_rows, precision=lax.Precision.HIGH...  88.1 us
    dot_general x8, matrix products, transform_planes(): return jnp.einsum('oxyz,ky->oxkz', field, cas_rows, precision=highest)  87.7 us
    dot_general x8, matrix products, transform_planes(): field = jnp.einsum('oxyz,kz->oxyk', field, cas_rows, precision=highest)  77.6 us
    all_to_all x4, local copies, waits for them, and re-layouts, per_device(): lax.all_to_all(spectrum, 'slab', split_axis=2, concat_axis=1, tiled=True)  39.5 us
    transpose x4, local copies, waits for them, and re-layouts, transform_planes(): return jnp.einsum('oxyz,ky->oxkz', field, cas_rows, precision=highest)  34 us
  transfers between devices with their start and end apart: 9, of which 9 were waited for; matrix products, arithmetic and copies ran while one was open for 28% of the time, Pallas kernels for 0%

commit v1 on v0

--- a/solution.py
+++ b/solution.py
@@ -10,7 +10,7 @@
 
 def broadcast(value, axis, source):
     kept = jnp.where(lax.axis_index(axis) == source, value, 0).astype(value.dtype)
-    return lax.psum(kept, axis)
+    return jnp.sum(lax.all_gather(kept, axis), axis=0)
 
 
 def cas_matrix(count):

time: 1170 us -> 1530 us (1.31)
  waiting for transfers between devices: 695 us -> 1020 us
  other arithmetic: 14.7 us -> 49.8 us
    all_gather x0 -> x4, waiting for transfers between devices: none -> 786 us  [broadcast(): return jnp.sum(lax.all_gather(kept, axis), axis=0)]
    psum x1 -> x0, waiting for transfers between devices: 275 us -> none  [broadcast(): return lax.psum(kept, axis)]
    all_to_all x4, waiting for transfers between devices: 249 us -> 49.1 us  [per_device(): lax.all_to_all(spectrum, 'slab', split_axis=2, concat_axis=1, tiled=True)]
    reduce_sum x0 -> x4, other arithmetic: none -> 32.4 us  [broadcast(): return jnp.sum(lax.all_gather(kept, axis), axis=0)]
  transfers between devices with their start and end apart: 9 -> 12, of which waited for: 9 -> 9; matrix products, arithmetic and copies ran while one was open for 28% -> 25% of each run, Pallas kernels for 0% -> 0%
where the time goes in v1:
time: 1530 us; the launch traced here: 1520 us
  waiting for transfers between devices  1020 us (67%)
  matrix products  256 us (17%)
  local copies, waits for them, and re-layouts  132 us (9%)
  other arithmetic  49.8 us (3%)
  starting transfers between devices  46.9 us (3%)
  between operations  24 us (2%)
    all_gather x4, waiting for transfers between devices, broadcast(): return jnp.sum(lax.all_gather(kept, axis), axis=0)  786 us
    all_to_all x4, waiting for transfers between devices, per_device(): lax.all_to_all(potential, 'slab', split_axis=1, concat_axis=2, tiled=True)  180 us
    dot_general x8, matrix products, transform_first(): jnp.einsum('oxyz,kx->okyz', field, cas_rows, precision=lax.Precision.HIGH...  87.8 us
    dot_general x8, matrix products, transform_planes(): return jnp.einsum('oxyz,ky->oxkz', field, cas_rows, precision=highest)  87.7 us
    dot_general x8, matrix products, transform_planes(): field = jnp.einsum('oxyz,kz->oxyk', field, cas_rows, precision=highest)  80.1 us
    all_to_all x4, waiting for transfers between devices, per_device(): lax.all_to_all(spectrum, 'slab', split_axis=2, concat_axis=1, tiled=True)  49.1 us
    all_to_all x4, local copies, waits for them, and re-layouts, per_device(): lax.all_to_all(spectrum, 'slab', split_axis=2, concat_axis=1, tiled=True)  40.2 us
    transpose x4, local copies, waits for them, and re-layouts, transform_planes(): return jnp.einsum('oxyz,ky->oxkz', field, cas_rows, precision=highest)  33.7 us
  transfers between devices with their start and end apart: 12, of which 9 were waited for; matrix products, arithmetic and copies ran while one was open for 25% of the time, Pallas kernels for 0%

profile of v1, /device:TPU:0, one launch (start us, length us, event | category | flops | bytes accessed | tf_op | source)
XLA Modules:
  0.0 1525.0 jit_solution(644770169376743500)
XLA Ops:
  29.2 228.4 %all-gather.11.cloned.1.call-done = f32[8,32,128,128]{3,2,1,0:T(8,128)} async-done(((f32[1,32,128,128]{3,2,1,0:T(8,128)}), f32[8,32,128,128]{3,2,1,0:T(8,128)}) %all-gather.11.cloned.1.call-update) | async-done | bytes 16777232 | tf_op jit(solution)/shard_map/all_gather | solution.py:13
  265.3 11.5 fusion.21
  299.6 185.9 %all-gather.9.cloned.1.call-done = f32[8,32,128,128]{3,2,1,0:T(8,128)} async-done(((f32[1,32,128,128]{3,2,1,0:T(8,128)}), f32[8,32,128,128]{3,2,1,0:T(8,128)}) %all-gather.9.cloned.1.call-update) | async-done | bytes 16777232 | tf_op jit(solution)/shard_map/all_gather | solution.py:13
  493.3 11.8 fusion.24
  527.9 185.6 %all-gather.7.cloned.1.call-done = f32[8,32,128,128]{3,2,1,0:T(8,128)} async-done(((f32[1,32,128,128]{3,2,1,0:T(8,128)}), f32[8,32,128,128]{3,2,1,0:T(8,128)}) %all-gather.7.cloned.1.call-update) | async-done | bytes 16777232 | tf_op jit(solution)/shard_map/all_gather | solution.py:13
  721.2 11.2 fusion.27
  755.2 186.1 %all-gather.5.cloned.1.call-done = f32[8,32,128,128]{3,2,1,0:T(8,128)} async-done(((f32[1,32,128,128]{3,2,1,0:T(8,128)}), f32[8,32,128,128]{3,2,1,0:T(8,128)}) %all-gather.5.cloned.1.call-update) | async-done | bytes 16777232 | tf_op jit(solution)/shard_map/all_gather | solution.py:13
  950.4 10.3 fusion.30
  987.2 10.6 copy.52
  997.8 12.8 fusion.12
  1027.9 49.1 %all-to-all-done = f32[4,32,128,128]{3,1,0,2:T(8,128)} async-done(((f32[4,32,128,128]{3,1,0,2:T(8,128)}), f32[4,32,128,128]{3,1,0,2:T(8,128)}, u32[]{:S(2)}, u32[]{:S(2)}) %all-to-all-start) | async-done | bytes 8388640 | tf_op jit(solution)/shard_map/all_to_all | solution.py:61
  1083.1 9.9 copy.45
  1092.9 12.8 fusion.14
  1123.3 52.5 %all-to-all-done.7 = f32[4,128,32,128]{3,2,0,1:T(8,128)} async-done(((f32[4,128,32,128]{3,2,0,1:T(8,128)}), f32[4,128,32,128]{3,2,0,1:T(8,128)}, u32[]{:S(2)}, u32[]{:S(2)}) %all-to-all-start.7) | async-done | bytes 8388640 | tf_op jit(solution)/shard_map/all_to_all | solution.py:64
  1181.9 9.9 copy.38
  1191.8 12.8 fusion.16
  1222.0 52.6 %all-to-all-done.5 = f32[4,128,32,128]{3,2,0,1:T(8,128)} async-done(((f32[4,128,32,128]{3,2,0,1:T(8,128)}), f32[4,128,32,128]{3,2,0,1:T(8,128)}, u32[]{:S(2)}, u32[]{:S(2)}) %all-to-all-start.5) | async-done | bytes 8388640 | tf_op jit(solution)/shard_map/all_to_all | solution.py:64
  1290.6 12.6 fusion.18
  1320.4 53.1 %all-to-all-done.3 = f32[4,128,32,128]{3,2,0,1:T(8,128)} async-done(((f32[4,128,32,128]{3,2,0,1:T(8,128)}), f32[4,128,32,128]{3,2,0,1:T(8,128)}, u32[]{:S(2)}, u32[]{:S(2)}) %all-to-all-start.3) | async-done | bytes 8388640 | tf_op jit(solution)/shard_map/all_to_all | solution.py:64
  1422.3 10.3 fusion.62
  1441.2 10.1 fusion.70
  1451.3 21.3 %all-to-all-done.1 = f32[4,128,32,128]{3,2,0,1:T(8,128)} async-done(((f32[4,128,32,128]{3,2,0,1:T(8,128)}), f32[4,128,32,128]{3,2,0,1:T(8,128)}, u32[]{:S(2)}, u32[]{:S(2)}) %all-to-all-start.1) | async-done | bytes 8388640 | tf_op jit(solution)/shard_map/all_to_all | solution.py:64
  1485.9 10.1 fusion.78
  1496.0 22.2 %fusion = f32[4,32,128,128]{3,2,1,0:T(8,128)} fusion(f32[128,4,32,128]{3,0,2,1:T(8,128)} %fusion.62, f32[128,4,32,128]{3,0,2,1:T(8,128)} %fusion.70, f32[128,4,32,128]{3,0,2,1:T(8,128)} %fusion.78, f32[32,128,128]{2,1,0:T(8,128)} %broadcast_multiply_fusion, f32[32,128,128]{2,1,0:T(8,128)} %broadcast_multiply_fusion.1, ...), kind=kOutput, calls=%fused_computation.1 | convolution fusion | flops 3238248448 | bytes 50331648 | tf_op jit(solution)/shard_map/oxyz,ky->oxkz/dot_general | solution.py:30
  (80 shorter events, 307.6 us)
Async XLA Ops:
  6.5 251.0 %all-gather.11.cloned.1.call-start = ((), (), s32[]{:S(2)}) async-start(), calls=%async_computation.11 | async-start | bytes 18874368 | tf_op jit(solution)/shard_map/all_gather | solution.py:13
  27.1 458.4 %all-gather.9.cloned.1.call-start = ((), (), s32[]{:S(2)}) async-start(), calls=%async_computation.10 | async-start | bytes 18874368 | tf_op jit(solution)/shard_map/all_gather | solution.py:13
  27.9 685.6 %all-gather.7.cloned.1.call-start = ((), (), s32[]{:S(2)}) async-start(), calls=%async_computation.9 | async-start | bytes 18874368 | tf_op jit(solution)/shard_map/all_gather | solution.py:13
  28.6 912.7 %all-gather.5.cloned.1.call-start = ((), (), s32[]{:S(2)}) async-start(), calls=%async_computation.8 | async-start | bytes 18874368 | tf_op jit(solution)/shard_map/all_gather | solution.py:13
  265.3 11.6 copy-start
  293.9 228.3 %all-to-all-start.6 = ((f32[4,32,128,128]{3,1,0,2:T(8,128)}), f32[4,32,128,128]{3,1,0,2:T(8,128)}, u32[]{:S(2)}, u32[]{:S(2)}) async-start(f32[4,32,128,128]{3,1,0,2:T(8,128)} %copy.50), calls=%async_computation.6 | async-start | bytes 16777216 | tf_op jit(solution)/shard_map/all_to_all | solution.py:61
  493.3 11.8 copy-start.2
  522.3 227.2 %all-to-all-start.4 = ((f32[4,32,128,128]{3,1,0,2:T(8,128)}), f32[4,32,128,128]{3,1,0,2:T(8,128)}, u32[]{:S(2)}, u32[]{:S(2)}) async-start(f32[4,32,128,128]{3,1,0,2:T(8,128)} %copy.43), calls=%async_computation.4 | async-start | bytes 16777216 | tf_op jit(solution)/shard_map/all_to_all | solution.py:61
  749.5 228.7 %all-to-all-start.2 = ((f32[4,32,128,128]{3,1,0,2:T(8,128)}), f32[4,32,128,128]{3,1,0,2:T(8,128)}, u32[]{:S(2)}, u32[]{:S(2)}) async-start(f32[4,32,128,128]{3,1,0,2:T(8,128)} %copy.36), calls=%async_computation.2 | async-start | bytes 16777216 | tf_op jit(solution)/shard_map/all_to_all | solution.py:61
  978.1 98.9 %all-to-all-start = ((f32[4,32,128,128]{3,1,0,2:T(8,128)}), f32[4,32,128,128]{3,1,0,2:T(8,128)}, u32[]{:S(2)}, u32[]{:S(2)}) async-start(f32[4,32,128,128]{3,1,0,2:T(8,128)} %copy.28), calls=%async_computation | async-start | bytes 16777216 | tf_op jit(solution)/shard_map/all_to_all | solution.py:61
  987.1 23.4 %copy-start.4 = (f32[128,32,128]{2,0,1:T(8,128)}, f32[128,32,128]{2,0,1:T(8,128)S(1)}, u32[]{:S(2)}) copy-start(f32[128,32,128]{2,0,1:T(8,128)S(1)} %copy.32) | copy-start | bytes 6291460
  1077.0 98.8 %all-to-all-start.7 = ((f32[4,128,32,128]{3,2,0,1:T(8,128)}), f32[4,128,32,128]{3,2,0,1:T(8,128)}, u32[]{:S(2)}, u32[]{:S(2)}) async-start(f32[4,128,32,128]{3,2,0,1:T(8,128)} %copy.54), calls=%async_computation.7 | async-start | bytes 16777216 | tf_op jit(solution)/shard_map/all_to_all | solution.py:64
  1092.9 12.8 copy-start.5
  1175.8 98.9 %all-to-all-start.5 = ((f32[4,128,32,128]{3,2,0,1:T(8,128)}), f32[4,128,32,128]{3,2,0,1:T(8,128)}, u32[]{:S(2)}, u32[]{:S(2)}) async-start(f32[4,128,32,128]{3,2,0,1:T(8,128)} %copy.47), calls=%async_computation.5 | async-start | bytes 16777216 | tf_op jit(solution)/shard_map/all_to_all | solution.py:64
  1191.8 12.8 copy-start.6
  1274.7 98.8 %all-to-all-start.3 = ((f32[4,128,32,128]{3,2,0,1:T(8,128)}), f32[4,128,32,128]{3,2,0,1:T(8,128)}, u32[]{:S(2)}, u32[]{:S(2)}) async-start(f32[4,128,32,128]{3,2,0,1:T(8,128)} %copy.40), calls=%async_computation.3 | async-start | bytes 16777216 | tf_op jit(solution)/shard_map/all_to_all | solution.py:64
  1290.6 12.6 copy-start.7
  1373.5 99.2 %all-to-all-start.1 = ((f32[4,128,32,128]{3,2,0,1:T(8,128)}), f32[4,128,32,128]{3,2,0,1:T(8,128)}, u32[]{:S(2)}, u32[]{:S(2)}) async-start(f32[4,128,32,128]{3,2,0,1:T(8,128)} %copy.33), calls=%async_computation.1 | async-start | bytes 16777216 | tf_op jit(solution)/shard_map/all_to_all | solution.py:64
  1379.5 4.8 copy-start.3
  1379.5 6.3 copy-start.1
  1404.4 9.3 copy-start.8
  1485.9 10.1 copy-start.9
Sparse Core Ops, SparseCore 0:
  27.2 230.2 all-gather.10
  259.7 225.7 all-gather.8
  487.6 225.7 all-gather.6
  715.4 225.7 all-gather.4
